TPU v7x, 512 devices: a whole 4x8x8 slice. The times are simulated.
512 devices in a mesh: row: 32 (over y, x), col: 16 (over z, core).
Axes of the slice: x: 4, y: 8, z: 8, core: 2. Of those that a mesh axis runs over, the one named last changes fastest.
Arguments:
- inputs: int32 [8, 128, 128], replicated, may hold values 0 or 1
- targets: int32 [8, 128, 128], replicated, may hold values 0 or 1
- initial_spikes: int32 [128, 128, 128], P(None, 'row'), may hold values 0 or 1
- w_in: bfloat16 [128, 128, 128], P(None, 'row'), may hold values from -0.5 to 0.5
- w_rec: bfloat16 [128, 128, 128, 128], P(None, 'col', 'row'), may hold values from -0.046875 to 0.046875
- w_out: bfloat16 [128, 128, 128], P('row'), may hold values from -0.046875 to 0.046875
- feedback: bfloat16 [128, 128, 128], P(None, 'row')
- adapt_gain: float32 [128, 128], P('row'), may hold values from 0.1 to 2
- adapt_decay: float32 [128, 128], P('row'), may hold values from 0.8 to 0.99
Outputs:
- readout: float32 [8, 128, 128], replicated
- grad_clipped: float32 [128, 128, 128, 128], P(None, 'col', 'row')
All inputs are finite; a program needn't handle non-finite values. No bound on the sum of `initial_spikes` on one device may be relied on, other than what follows from the above.
Results may differ from a plain program's by a relative error of at most 0.0015.
Values may be sent and summed in bfloat16 or wider, within the bound.
A program may use at most 128 MiB of HBM per device.

v0:
```python
import functools

import jax
import jax.numpy as jnp
from jax import lax
from jax.sharding import Mesh
from jax.sharding import PartitionSpec as P

NA = 128
NB = 128
COL = ("col_0", "col_1")
ROW = ("row_0", "row_1")
ROW_COL = ("row_0", "row_1", "col_0", "col_1")


cellular_leak_multiplier = 0.8
readout_decay = 0.8


def cut_along(array, dim, length):
    before, after = (array.shape[:dim], array.shape[dim + 1 :])
    return jnp.moveaxis(array.reshape(*before, length, -1, *after), dim, 0)


def sum_at_owner(array, axis, dim):
    length = lax.axis_size(axis)
    pieces = lax.all_to_all(cut_along(array, dim, length), axis, 0, 0, tiled=True)
    return jnp.sum(pieces, axis=0)


def laid_out(pieces, dim):
    shape = list(pieces.shape[1:])
    shape[dim] *= pieces.shape[0]
    return jnp.moveaxis(pieces, 0, dim).reshape(shape)


def sent_to_all(array, axis):
    copies = jnp.broadcast_to(array, (lax.axis_size(axis), *array.shape))
    return lax.all_to_all(copies, axis, split_axis=0, concat_axis=0, tiled=True)


def collect(array, axis, dim):
    return laid_out(sent_to_all(array, axis), dim)


def summed_rows(array, axes, dim):
    far, near = axes
    own = sum_at_owner(cut_along(array, dim, lax.axis_size(far)), near, dim + 1)
    return jnp.sum(lax.all_to_all(own, far, 0, 0, tiled=True), axis=0)


def rows_for(lines, length):
    spare = -lines.shape[0] % length
    if not spare:
        return lines
    return jnp.concatenate([lines, jnp.zeros((spare, *lines.shape[1:]), lines.dtype)])


def whole_of(array, axes, dim):
    far, near = axes
    pieces = sent_to_all(sent_to_all(array, far), near)
    return laid_out(pieces.swapaxes(0, 1).reshape(-1, *array.shape), dim)


def nested_sum(array, axes):
    lines = array.reshape(-1, array.shape[-1])
    own = summed_rows(rows_for(lines, lax.axis_size(axes[0]) * lax.axis_size(axes[1])), axes, 0)
    whole = whole_of(own, axes, 0)
    return whole[: len(lines)].reshape(array.shape)


def by_axis(array, axes):
    return functools.reduce(lax.psum, axes, array)


def body(inputs, targets, initial_spikes, w_in, w_rec, w_out, feedback, adapt_gain, adapt_decay):
    steps_count, batch, channels = inputs.shape
    own_cols = w_rec.shape[1]
    rows_loc = w_rec.shape[2]
    entire_column_set = w_rec.shape[3]
    col_start = lax.axis_index(COL) * own_cols
    rows_all = steps_count * batch

    def own_part(array, axis_dim):
        return lax.dynamic_slice_in_dim(array, col_start, own_cols, axis_dim)

    def select_cols(array, axis_dim):
        return own_part(array, axis_dim)

    def combine_currents(partial_value):
        return sum_at_owner(partial_value, COL, 2)

    weights = w_rec.reshape(w_rec.shape[0] * own_cols, rows_loc * entire_column_set)
    w_in_loc = select_cols(w_in, 2)
    state_cols = w_in_loc.shape[2]
    external = jnp.dot(
        inputs.reshape(rows_all, channels).astype(jnp.bfloat16),
        w_in_loc.reshape(channels, -1),
        preferred_element_type=jnp.float32,
    ).reshape(steps_count, batch, rows_loc, state_cols)
    coupling_magnitude = select_cols(adapt_gain, 1)
    retention = select_cols(adapt_decay, 1)
    start_spikes = select_cols(initial_spikes, 2).astype(jnp.bfloat16)

    def advance(state, drive_now):
        pulse_output, cellular_charge, barrier_shift_amount, sender_trace = state
        arrivals = collect(pulse_output, ROW, 1).reshape(batch, -1)
        sender_trace = cellular_leak_multiplier * sender_trace + arrivals.astype(jnp.float32)
        partial_value = jnp.dot(arrivals, weights, preferred_element_type=jnp.float32).reshape(
            batch, rows_loc, entire_column_set
        )
        current = drive_now + combine_currents(partial_value)
        spike_float = pulse_output.astype(jnp.float32)
        cellular_charge = cellular_leak_multiplier * cellular_charge + current - spike_float
        barrier_shift_amount = retention * barrier_shift_amount + spike_float
        present_emission_frequency = jax.nn.sigmoid(
            cellular_charge - 1.0 - coupling_magnitude * barrier_shift_amount
        )
        surrogate_slope = present_emission_frequency * (1.0 - present_emission_frequency)
        pulse_output = present_emission_frequency.astype(jnp.bfloat16)
        return (
            (pulse_output, cellular_charge, barrier_shift_amount, sender_trace),
            (sender_trace.astype(jnp.bfloat16), surrogate_slope, pulse_output),
        )

    zeros = jnp.zeros((batch, rows_loc, state_cols), jnp.float32)
    trace_zero = jnp.zeros((batch, weights.shape[0]), jnp.float32)
    _, (traces, slopes, spikes) = lax.scan(
        advance, (start_spikes, zeros, zeros, trace_zero), external
    )
    readout_loc = own_part(w_out, 1).reshape(rows_loc * own_cols, -1)
    projected = nested_sum(
        jnp.dot(spikes.reshape(rows_all, -1), readout_loc, preferred_element_type=jnp.float32),
        ("row_0", ("row_1", "col_0", "col_1")),
    )
    outputs_n = readout_loc.shape[1]
    projected = projected.reshape(steps_count, batch, outputs_n)

    def smooth(level, incoming):
        level = readout_decay * level + incoming
        return (level, level)

    _, readout = lax.scan(smooth, jnp.zeros((batch, outputs_n), jnp.float32), projected)
    errors = (jax.nn.sigmoid(readout) - targets.astype(jnp.float32)).reshape(rows_all, outputs_n)
    err_high = errors.astype(jnp.bfloat16)
    err_low = (errors - err_high.astype(jnp.float32)).astype(jnp.bfloat16)
    feedback_loc = select_cols(feedback, 2).reshape(outputs_n, -1)
    signal = jnp.dot(err_high, feedback_loc, preferred_element_type=jnp.float32) + jnp.dot(
        err_low, feedback_loc, preferred_element_type=jnp.float32
    )
    signal = signal.reshape(steps_count, batch, rows_loc, state_cols)
    weighted = signal * slopes
    decays = retention - slopes * coupling_magnitude

    def backward(carried, inputs_now):
        weighted_now, decay_now = inputs_now
        return (weighted_now + decay_now * carried, carried)

    _, future = lax.scan(backward, zeros, (weighted, decays), reverse=True)
    factors = (weighted - coupling_magnitude * slopes * future).astype(jnp.bfloat16)
    traces_flat = traces.reshape(rows_all, -1)
    pieces = lax.all_gather(
        factors.reshape(rows_all, rows_loc, state_cols), COL, axis=2, tiled=True
    )
    product = lax.dot_general(
        traces_flat,
        pieces.reshape(rows_all, -1),
        (((0,), (0,)), ((), ())),
        preferred_element_type=jnp.float32,
    )
    grad = product.reshape(-1, rows_loc, pieces.shape[2])
    squares = by_axis(jnp.sum(grad * grad), ROW_COL)
    clip_factor = jnp.minimum(1.0, NA * NB / 16.0 / jnp.sqrt(squares + 1e-06))
    return (readout, (grad * clip_factor).reshape(w_rec.shape))


def solution(mesh):
    finer = Mesh(mesh.devices.reshape(8, 4, 8, 2), ("row_0", "row_1", "col_0", "col_1"))
    placed = (
        P(),
        P(),
        P(None, ROW, None),
        P(None, ROW, None),
        P(None, COL, ROW, None),
        P(ROW, None, None),
        P(None, ROW, None),
        P(ROW, None),
        P(ROW, None),
    )
    return jax.shard_map(
        body, mesh=finer, in_specs=placed, out_specs=(P(), P(None, COL, ROW, None)), check_vma=False
    )
```

profile of v0, /device:TPU:1, one launch (start us, length us, event | category | flops | bytes accessed | tf_op | source)
XLA Modules:
  0.0 466.9 jit_solution(16170017238563502800)
XLA Ops:
  7.3 1.1 constant_dynamic-slice_fusion.4
  8.5 1.1 convert_element_type.57
  11.0 286.9 %while.55 = (s32[]{:T(128)}, bf16[128,4,8]{0,2,1:T(8,128)(2,1)S(1)}, f32[128,4,8]{0,2,1:T(8,128)S(1)}, f32[128,4,8]{0,2,1:T(8,128)S(1)}, f32[128,1024]{0,1:T(8,1...) while((s32[]{:T(128)}, ...), condition=%wide.region_2.3_spmd.clone, body=%wide.region_0.2_spmd.clone.sunk | while | flops 135032832 | bytes 6756560 | solution.py:128
  11.0 21.5 %all_to_all.41 = bf16[32,128,4,8]{1,3,2,0:T(8,128)(2,1)S(1)} all-to-all(bf16[32,128,4,8]{1,3,2,0:T(8,128)(2,1)S(1)} %broadcast_in_dim.84), channel_id=1, replica_groups=mesh['row_0'=8,'row_1'=4,'col_0'=8,'col_1'=2] {'row_0','row_1'}, dimensions={0} | all-to-all | bytes 524288 | tf_op jit(solution)/shard_map/while/body/eval_jaxpr/all_to_all | solution.py:39
  32.5 0.7 convolution_bitcast_fusion.4
  33.2 0.8 copy.144
  34.0 12.8 %all-to-all-start.1 = ((f32[16,128,4,8]{1,3,2,0:T(8,128)}), f32[16,128,4,8]{1,3,2,0:T(8,128)S(1)}, u32[]{:S(2)}, u32[]{:S(2)}) async-start(f32[16,128,4,8]{1,3,2,0:T(8,128)} %copy.144), calls=%async_computation.1 | async-start | bytes 524288 | tf_op jit(solution)/shard_map/while/body/eval_jaxpr/all_to_all | solution.py:27
  47.3 0.7 constant_dynamic-update-slice_fusion.2
  48.0 10.5 %all-to-all-done.1 = f32[16,128,4,8]{1,3,2,0:T(8,128)S(1)} async-done(((f32[16,128,4,8]{1,3,2,0:T(8,128)}), f32[16,128,4,8]{1,3,2,0:T(8,128)S(1)}, u32[]{:S(2)}, u32[]{:S(2)}) %all-to-all-start.1) | async-done | bytes 262176 | tf_op jit(solution)/shard_map/while/body/eval_jaxpr/all_to_all | solution.py:27
  58.8 16.4 %all_to_all.41 = bf16[32,128,4,8]{1,3,2,0:T(8,128)(2,1)S(1)} all-to-all(bf16[32,128,4,8]{1,3,2,0:T(8,128)(2,1)S(1)} %broadcast_in_dim.84), channel_id=1, replica_groups=mesh['row_0'=8,'row_1'=4,'col_0'=8,'col_1'=2] {'row_0','row_1'}, dimensions={0} | all-to-all | bytes 524288 | tf_op jit(solution)/shard_map/while/body/eval_jaxpr/all_to_all | solution.py:39
  75.2 0.7 convolution_bitcast_fusion.4
  75.9 0.8 copy.144
  76.7 4.0 all-to-all-start.1
  81.2 0.7 constant_dynamic-update-slice_fusion.2
  82.0 10.6 %all-to-all-done.1 = f32[16,128,4,8]{1,3,2,0:T(8,128)S(1)} async-done(((f32[16,128,4,8]{1,3,2,0:T(8,128)}), f32[16,128,4,8]{1,3,2,0:T(8,128)S(1)}, u32[]{:S(2)}, u32[]{:S(2)}) %all-to-all-start.1) | async-done | bytes 262176 | tf_op jit(solution)/shard_map/while/body/eval_jaxpr/all_to_all | solution.py:27
  92.9 16.7 %all_to_all.41 = bf16[32,128,4,8]{1,3,2,0:T(8,128)(2,1)S(1)} all-to-all(bf16[32,128,4,8]{1,3,2,0:T(8,128)(2,1)S(1)} %broadcast_in_dim.84), channel_id=1, replica_groups=mesh['row_0'=8,'row_1'=4,'col_0'=8,'col_1'=2] {'row_0','row_1'}, dimensions={0} | all-to-all | bytes 524288 | tf_op jit(solution)/shard_map/while/body/eval_jaxpr/all_to_all | solution.py:39
  110.2 0.8 copy.144
  111.0 3.7 all-to-all-start.1
  115.3 0.7 constant_dynamic-update-slice_fusion.2
  116.0 10.6 %all-to-all-done.1 = f32[16,128,4,8]{1,3,2,0:T(8,128)S(1)} async-done(((f32[16,128,4,8]{1,3,2,0:T(8,128)}), f32[16,128,4,8]{1,3,2,0:T(8,128)S(1)}, u32[]{:S(2)}, u32[]{:S(2)}) %all-to-all-start.1) | async-done | bytes 262176 | tf_op jit(solution)/shard_map/while/body/eval_jaxpr/all_to_all | solution.py:27
  126.9 16.9 %all_to_all.41 = bf16[32,128,4,8]{1,3,2,0:T(8,128)(2,1)S(1)} all-to-all(bf16[32,128,4,8]{1,3,2,0:T(8,128)(2,1)S(1)} %broadcast_in_dim.84), channel_id=1, replica_groups=mesh['row_0'=8,'row_1'=4,'col_0'=8,'col_1'=2] {'row_0','row_1'}, dimensions={0} | all-to-all | bytes 524288 | tf_op jit(solution)/shard_map/while/body/eval_jaxpr/all_to_all | solution.py:39
  143.8 0.7 convolution_bitcast_fusion.4
  144.4 0.8 copy.144
  145.2 3.7 all-to-all-start.1
  149.5 0.7 constant_dynamic-update-slice_fusion.2
  150.2 10.6 %all-to-all-done.1 = f32[16,128,4,8]{1,3,2,0:T(8,128)S(1)} async-done(((f32[16,128,4,8]{1,3,2,0:T(8,128)}), f32[16,128,4,8]{1,3,2,0:T(8,128)S(1)}, u32[]{:S(2)}, u32[]{:S(2)}) %all-to-all-start.1) | async-done | bytes 262176 | tf_op jit(solution)/shard_map/while/body/eval_jaxpr/all_to_all | solution.py:27
  161.1 16.9 %all_to_all.41 = bf16[32,128,4,8]{1,3,2,0:T(8,128)(2,1)S(1)} all-to-all(bf16[32,128,4,8]{1,3,2,0:T(8,128)(2,1)S(1)} %broadcast_in_dim.84), channel_id=1, replica_groups=mesh['row_0'=8,'row_1'=4,'col_0'=8,'col_1'=2] {'row_0','row_1'}, dimensions={0} | all-to-all | bytes 524288 | tf_op jit(solution)/shard_map/while/body/eval_jaxpr/all_to_all | solution.py:39
  178.6 0.8 copy.144
  179.4 3.7 all-to-all-start.1
  183.7 0.7 constant_dynamic-update-slice_fusion.2
  184.4 10.6 %all-to-all-done.1 = f32[16,128,4,8]{1,3,2,0:T(8,128)S(1)} async-done(((f32[16,128,4,8]{1,3,2,0:T(8,128)}), f32[16,128,4,8]{1,3,2,0:T(8,128)S(1)}, u32[]{:S(2)}, u32[]{:S(2)}) %all-to-all-start.1) | async-done | bytes 262176 | tf_op jit(solution)/shard_map/while/body/eval_jaxpr/all_to_all | solution.py:27
  195.3 16.9 %all_to_all.41 = bf16[32,128,4,8]{1,3,2,0:T(8,128)(2,1)S(1)} all-to-all(bf16[32,128,4,8]{1,3,2,0:T(8,128)(2,1)S(1)} %broadcast_in_dim.84), channel_id=1, replica_groups=mesh['row_0'=8,'row_1'=4,'col_0'=8,'col_1'=2] {'row_0','row_1'}, dimensions={0} | all-to-all | bytes 524288 | tf_op jit(solution)/shard_map/while/body/eval_jaxpr/all_to_all | solution.py:39
  212.2 0.7 convolution_bitcast_fusion.4
  212.9 0.8 copy.144
  213.6 3.7 all-to-all-start.1
  217.9 0.7 constant_dynamic-update-slice_fusion.2
  218.6 10.6 %all-to-all-done.1 = f32[16,128,4,8]{1,3,2,0:T(8,128)S(1)} async-done(((f32[16,128,4,8]{1,3,2,0:T(8,128)}), f32[16,128,4,8]{1,3,2,0:T(8,128)S(1)}, u32[]{:S(2)}, u32[]{:S(2)}) %all-to-all-start.1) | async-done | bytes 262176 | tf_op jit(solution)/shard_map/while/body/eval_jaxpr/all_to_all | solution.py:27
  229.5 16.9 %all_to_all.41 = bf16[32,128,4,8]{1,3,2,0:T(8,128)(2,1)S(1)} all-to-all(bf16[32,128,4,8]{1,3,2,0:T(8,128)(2,1)S(1)} %broadcast_in_dim.84), channel_id=1, replica_groups=mesh['row_0'=8,'row_1'=4,'col_0'=8,'col_1'=2] {'row_0','row_1'}, dimensions={0} | all-to-all | bytes 524288 | tf_op jit(solution)/shard_map/while/body/eval_jaxpr/all_to_all | solution.py:39
  247.1 0.8 copy.144
  247.8 3.7 all-to-all-start.1
  252.1 0.7 constant_dynamic-update-slice_fusion.2
  252.8 10.6 %all-to-all-done.1 = f32[16,128,4,8]{1,3,2,0:T(8,128)S(1)} async-done(((f32[16,128,4,8]{1,3,2,0:T(8,128)}), f32[16,128,4,8]{1,3,2,0:T(8,128)S(1)}, u32[]{:S(2)}, u32[]{:S(2)}) %all-to-all-start.1) | async-done | bytes 262176 | tf_op jit(solution)/shard_map/while/body/eval_jaxpr/all_to_all | solution.py:27
  263.7 16.9 %all_to_all.41 = bf16[32,128,4,8]{1,3,2,0:T(8,128)(2,1)S(1)} all-to-all(bf16[32,128,4,8]{1,3,2,0:T(8,128)(2,1)S(1)} %broadcast_in_dim.84), channel_id=1, replica_groups=mesh['row_0'=8,'row_1'=4,'col_0'=8,'col_1'=2] {'row_0','row_1'}, dimensions={0} | all-to-all | bytes 524288 | tf_op jit(solution)/shard_map/while/body/eval_jaxpr/all_to_all | solution.py:39
  281.3 0.8 copy.144
  282.0 3.7 all-to-all-start.1
  286.3 0.7 constant_dynamic-update-slice_fusion.2
  287.0 10.6 %all-to-all-done.1 = f32[16,128,4,8]{1,3,2,0:T(8,128)S(1)} async-done(((f32[16,128,4,8]{1,3,2,0:T(8,128)}), f32[16,128,4,8]{1,3,2,0:T(8,128)S(1)}, u32[]{:S(2)}, u32[]{:S(2)}) %all-to-all-start.1) | async-done | bytes 262176 | tf_op jit(solution)/shard_map/while/body/eval_jaxpr/all_to_all | solution.py:27
  297.9 0.9 copy.105
  299.3 0.9 convolution_bitcast_fusion.1
  300.6 22.0 %all_to_all.42 = f32[64,8,2,128]{3,2,1,0:T(2,128)S(1)} all-to-all(f32[64,8,2,128]{3,2,1,0:T(2,128)S(1)} %copy.107), channel_id=1, replica_groups=mesh['row_0'=8,'row_1'=4,'col_0'=8,'col_1'=2] {'row_1','col_0','col_1'}, dimensions={0} | all-to-all | bytes 1048576 | tf_op jit(solution)/shard_map/all_to_all | solution.py:27
  322.8 8.9 %all_to_all.43 = f32[8,2,128]{2,1,0:T(2,128)S(1)} all-to-all(f32[8,2,128]{2,1,0:T(2,128)S(1)} %reduce_sum.39), channel_id=1, replica_groups=mesh['row_0'=8,'row_1'=4,'col_0'=8,'col_1'=2] {'row_0'}, dimensions={0} | all-to-all | bytes 16384 | tf_op jit(solution)/shard_map/all_to_all | solution.py:49
  331.8 8.9 %all_to_all.40 = f32[8,2,128]{2,1,0:T(2,128)S(1)} all-to-all(f32[8,2,128]{2,1,0:T(2,128)S(1)} %broadcast_in_dim.75), channel_id=1, replica_groups=mesh['row_0'=8,'row_1'=4,'col_0'=8,'col_1'=2] {'row_0'}, dimensions={0} | all-to-all | bytes 16384 | tf_op jit(solution)/shard_map/all_to_all | solution.py:39
  340.7 0.9 broadcast_in_dim.76
  341.6 8.7 %all-to-all-start.5 = ((f32[64,8,2,128]{3,2,1,0:T(2,128)}), f32[64,8,2,128]{3,2,1,0:T(2,128)S(1)}, u32[]{:S(2)}, u32[]{:S(2)}) async-start(f32[64,8,2,128]{3,2,1,0:T(2,128)} %broadcast_in_dim.76), calls=%async_computation.5 | async-start | bytes 1048576 | tf_op jit(solution)/shard_map/all_to_all | solution.py:39
  350.7 17.0 %all-to-all-done.5 = f32[64,8,2,128]{3,2,1,0:T(2,128)S(1)} async-done(((f32[64,8,2,128]{3,2,1,0:T(2,128)}), f32[64,8,2,128]{3,2,1,0:T(2,128)S(1)}, u32[]{:S(2)}, u32[]{:S(2)}) %all-to-all-start.5) | async-done | bytes 524320 | tf_op jit(solution)/shard_map/all_to_all | solution.py:39
  367.7 0.9 while.56
  369.8 0.7 copy_bitcast_fusion.1
  370.5 34.3 %all-gather.2.cloned.1.call-done = bf16[1024,4,128]{0,2,1:T(8,128)(2,1)} async-done(((bf16[1024,4,8]{0,2,1:T(8,128)(2,1)}), bf16[1024,4,128]{0,2,1:T(8,128)(2,1)}) %all-gather.2.cloned.1.call-update) | async-done | bytes 1048592 | tf_op jit(solution)/shard_map/all_gather | solution.py:162
  404.8 4.0 multiply_reduce_fusion
  408.8 14.1 %psum.28 = f32[]{:T(128)} all-reduce(f32[]{:T(128)} %get-tuple-element.519), channel_id=1, replica_groups=mesh['row_0'=8,'row_1'=4,'col_0'=8,'col_1'=2] {'row_0'}, use_global_device_ids=true, to_apply=%region_10.11 | all-reduce | flops 1 | bytes 8 | tf_op jit(solution)/shard_map/psum | solution.py:73
  422.9 9.0 %psum.29 = f32[]{:T(128)} all-reduce(f32[]{:T(128)} %psum.28), channel_id=1, replica_groups=mesh['row_0'=8,'row_1'=4,'col_0'=8,'col_1'=2] {'row_1'}, use_global_device_ids=true, to_apply=%region_11.12 | all-reduce | flops 1 | bytes 8 | tf_op jit(solution)/shard_map/psum | solution.py:73
  431.9 12.4 %psum.30 = f32[]{:T(128)} all-reduce(f32[]{:T(128)} %psum.29), channel_id=1, replica_groups=mesh['row_0'=8,'row_1'=4,'col_0'=8,'col_1'=2] {'col_0'}, use_global_device_ids=true, to_apply=%region_12.13 | all-reduce | flops 1 | bytes 8 | tf_op jit(solution)/shard_map/psum | solution.py:73
  444.2 12.3 %psum.31 = f32[]{:T(128)} all-reduce(f32[]{:T(128)} %psum.30), channel_id=1, replica_groups=mesh['row_0'=8,'row_1'=4,'col_0'=8,'col_1'=2] {'col_1'}, use_global_device_ids=true, to_apply=%region_13.14 | all-reduce | flops 1 | bytes 8 | tf_op jit(solution)/shard_map/psum | solution.py:73
  457.4 2.7 copy.116
  (132 shorter events, 13.9 us)
Async XLA Ops:
  7.2 2.4 copy-start
  7.2 2.7 copy-start.1
  9.9 0.8 copy-start.5
  9.9 0.8 copy-start.6
  34.0 24.5 %all-to-all-start.1 = ((f32[16,128,4,8]{1,3,2,0:T(8,128)}), f32[16,128,4,8]{1,3,2,0:T(8,128)S(1)}, u32[]{:S(2)}, u32[]{:S(2)}) async-start(f32[16,128,4,8]{1,3,2,0:T(8,128)} %copy.144), calls=%async_computation.1 | async-start | bytes 524288 | tf_op jit(solution)/shard_map/while/body/eval_jaxpr/all_to_all | solution.py:27
  76.7 15.9 %all-to-all-start.1 = ((f32[16,128,4,8]{1,3,2,0:T(8,128)}), f32[16,128,4,8]{1,3,2,0:T(8,128)S(1)}, u32[]{:S(2)}, u32[]{:S(2)}) async-start(f32[16,128,4,8]{1,3,2,0:T(8,128)} %copy.144), calls=%async_computation.1 | async-start | bytes 524288 | tf_op jit(solution)/shard_map/while/body/eval_jaxpr/all_to_all | solution.py:27
  111.0 15.6 %all-to-all-start.1 = ((f32[16,128,4,8]{1,3,2,0:T(8,128)}), f32[16,128,4,8]{1,3,2,0:T(8,128)S(1)}, u32[]{:S(2)}, u32[]{:S(2)}) async-start(f32[16,128,4,8]{1,3,2,0:T(8,128)} %copy.144), calls=%async_computation.1 | async-start | bytes 524288 | tf_op jit(solution)/shard_map/while/body/eval_jaxpr/all_to_all | solution.py:27
  145.2 15.6 %all-to-all-start.1 = ((f32[16,128,4,8]{1,3,2,0:T(8,128)}), f32[16,128,4,8]{1,3,2,0:T(8,128)S(1)}, u32[]{:S(2)}, u32[]{:S(2)}) async-start(f32[16,128,4,8]{1,3,2,0:T(8,128)} %copy.144), calls=%async_computation.1 | async-start | bytes 524288 | tf_op jit(solution)/shard_map/while/body/eval_jaxpr/all_to_all | solution.py:27
  179.4 15.6 %all-to-all-start.1 = ((f32[16,128,4,8]{1,3,2,0:T(8,128)}), f32[16,128,4,8]{1,3,2,0:T(8,128)S(1)}, u32[]{:S(2)}, u32[]{:S(2)}) async-start(f32[16,128,4,8]{1,3,2,0:T(8,128)} %copy.144), calls=%async_computation.1 | async-start | bytes 524288 | tf_op jit(solution)/shard_map/while/body/eval_jaxpr/all_to_all | solution.py:27
  213.6 15.6 %all-to-all-start.1 = ((f32[16,128,4,8]{1,3,2,0:T(8,128)}), f32[16,128,4,8]{1,3,2,0:T(8,128)S(1)}, u32[]{:S(2)}, u32[]{:S(2)}) async-start(f32[16,128,4,8]{1,3,2,0:T(8,128)} %copy.144), calls=%async_computation.1 | async-start | bytes 524288 | tf_op jit(solution)/shard_map/while/body/eval_jaxpr/all_to_all | solution.py:27
  247.8 15.6 %all-to-all-start.1 = ((f32[16,128,4,8]{1,3,2,0:T(8,128)}), f32[16,128,4,8]{1,3,2,0:T(8,128)S(1)}, u32[]{:S(2)}, u32[]{:S(2)}) async-start(f32[16,128,4,8]{1,3,2,0:T(8,128)} %copy.144), calls=%async_computation.1 | async-start | bytes 524288 | tf_op jit(solution)/shard_map/while/body/eval_jaxpr/all_to_all | solution.py:27
  282.0 15.6 %all-to-all-start.1 = ((f32[16,128,4,8]{1,3,2,0:T(8,128)}), f32[16,128,4,8]{1,3,2,0:T(8,128)S(1)}, u32[]{:S(2)}, u32[]{:S(2)}) async-start(f32[16,128,4,8]{1,3,2,0:T(8,128)} %copy.144), calls=%async_computation.1 | async-start | bytes 524288 | tf_op jit(solution)/shard_map/while/body/eval_jaxpr/all_to_all | solution.py:27
  300.2 50.2 %copy-start.4 = (bf16[128,4,128]{2,1,0:T(4,128)(2,1)S(1)}, bf16[128,4,128]{2,1,0:T(4,128)(2,1)}, u32[]{:S(2)}) copy-start(bf16[128,4,128]{2,1,0:T(4,128)(2,1)} %param.21) | copy-start | bytes 393220
  341.6 27.0 %copy-start.2 = (s32[8,128,128]{2,1,0:T(8,128)S(1)}, s32[8,128,128]{2,1,0:T(8,128)}, u32[]{:S(2)}) copy-start(s32[8,128,128]{2,1,0:T(8,128)} %param.16) | copy-start | bytes 1572868
  341.6 26.0 %all-to-all-start.5 = ((f32[64,8,2,128]{3,2,1,0:T(2,128)}), f32[64,8,2,128]{3,2,1,0:T(2,128)S(1)}, u32[]{:S(2)}, u32[]{:S(2)}) async-start(f32[64,8,2,128]{3,2,1,0:T(2,128)} %broadcast_in_dim.76), calls=%async_computation.5 | async-start | bytes 1048576 | tf_op jit(solution)/shard_map/all_to_all | solution.py:39
  350.3 54.5 %all-gather.2.cloned.1.call-start = ((), (), s32[]{:S(2)}) async-start(), calls=%async_computation.6 | async-start | bytes 1114112 | tf_op jit(solution)/shard_map/all_gather | solution.py:162
  368.6 1.9 copy-start.3
Sparse Core Ops, SparseCore 0:
  370.7 34.1 all-gather.1
where the time goes:
time: 469 us; the launch traced here: 467 us
  blocking collectives  226 us (48%)
  waiting for transfers between devices  136 us (29%)
  starting transfers between devices  47.9 us (10%)
  local copies, waits for them, and re-layouts  22 us (5%)
  between operations  15 us (3%)
  matrix products  10.9 us (2%)
  other arithmetic  7.65 us (2%)
    all_to_all x9, blocking collectives, sent_to_all(): return lax.all_to_all(copies, axis, split_axis=0, concat_axis=0, tiled=True)  148 us
    all_to_all x8, waiting for transfers between devices, sum_at_owner(): lax.all_to_all(cut_along(array, dim, length), axis, 0, 0, tiled=True)  84.7 us
    psum x4, blocking collectives, by_axis(): return functools.reduce(lax.psum, axes, array)  47.7 us
    all_to_all x8, starting transfers between devices, sum_at_owner(): lax.all_to_all(cut_along(array, dim, length), axis, 0, 0, tiled=True)  39.1 us
    all_gather x1, waiting for transfers between devices, body(): lax.all_gather(factors.reshape(rows_all, rows_loc, state_cols), COL, axis...  34.3 us
    all_to_all x1, blocking collectives, sum_at_owner(): lax.all_to_all(cut_along(array, dim, length), axis, 0, 0, tiled=True)  22 us
    all_to_all x1, waiting for transfers between devices, sent_to_all(): return lax.all_to_all(copies, axis, split_axis=0, concat_axis=0, tiled=True)  17 us
  transfers between devices with their start and end apart: 10, of which 10 were waited for; matrix products, arithmetic and copies ran while one was open for 2% of the time, Pallas kernels for 0%

commit v1 on v0

v1 whole, which is shorter than its diff:
```python
import functools

import jax
import jax.numpy as jnp
from jax import lax
from jax.experimental import pallas as pl
from jax.experimental.pallas import tpu as pltpu
from jax.sharding import PartitionSpec as P

MESH = pl.DeviceIdType.MESH
LEAK = 0.8
READ_DECAY = 0.8
F32 = jnp.float32
BF16 = jnp.bfloat16


def outward(i, n):
    return n // 2 + (1 - 2 * (i % 2)) * ((i + 1) // 2)


def kernel(dims, wt, fbt, gain, decay, s0, wint, inp, tgt, wo, grad, readout, clip,
           S, F, CS, CR, CT, ext, v, u, PS, PR, QS, QR, RO, rd, TR, tr, SL, WG, FT, sq, N1, N2,
           s_sem, f_sem, c_sem, p_sem, q_sem, r_sem, n_sem):
    ny, nx, nz, nk, nb, steps, neurons = dims
    rows, cols = ny * nx, nz * nk
    r, c = lax.axis_index("row"), lax.axis_index("col")
    y, x, z, k = r // nx, r % nx, c // nk, c % nk
    own = s0.shape[0]
    batch = s0.shape[1]
    ns, nr = wt.shape[1], wt.shape[0]
    kn = tgt.shape[1]
    kp = kn // cols
    groups = nr // nb

    def row_peer(j):
        return ((y + outward(j // nx, ny)) % ny) * nx + (x + outward(j % nx, nx)) % nx

    def col_peer(j):
        return ((z + outward(j // nk, nz)) % nz) * nk + (k + outward(j % nk, nk)) % nk

    def to_rows(fn, sem):
        def one(j, _):
            p = row_peer(j)
            src, dst = fn(p)
            pltpu.make_async_remote_copy(src_ref=src, dst_ref=dst, send_sem=sem.at[0], recv_sem=sem.at[1],
                                         device_id=(p, c), device_id_type=MESH).start()
            return 0
        lax.fori_loop(0, rows - 1, one, 0)

    def to_cols(fn, sem):
        def one(j, _):
            p = col_peer(j)
            src, dst = fn(p)
            pltpu.make_async_remote_copy(src_ref=src, dst_ref=dst, send_sem=sem.at[0], recv_sem=sem.at[1],
                                         device_id=(r, p), device_id_type=MESH).start()
            return 0
        lax.fori_loop(0, cols - 1, one, 0)

    def settle(ref, sem):
        pltpu.make_async_copy(ref, ref, sem).wait()

    barrier = pltpu.get_barrier_semaphore()

    def greet_row(j, _):
        pl.semaphore_signal(barrier, inc=1, device_id=(row_peer(j), c), device_id_type=MESH)
        return 0

    def greet_col(j, _):
        pl.semaphore_signal(barrier, inc=1, device_id=(r, col_peer(j)), device_id_type=MESH)
        return 0

    lax.fori_loop(0, rows - 1, greet_row, 0)
    lax.fori_loop(0, cols - 1, greet_col, 0)

    own_rows = pl.ds(pl.multiple_of(r * own, own), own)
    own_k = pl.ds(pl.multiple_of(c * kp, kp), kp)

    def piece(ref):
        return jnp.concatenate([ref[pl.ds(pl.multiple_of(a * nb + c * 8, 8), 8), :] for a in range(groups)], axis=0)

    g_own, d_own = piece(gain), piece(decay)
    for t in range(steps):
        ext[t] = lax.dot_general(wint[...], inp[t], (((1,), (1,)), ((), ())), preferred_element_type=F32)
    v[...] = jnp.zeros_like(v)
    u[...] = jnp.zeros_like(u)
    tr[...] = jnp.zeros_like(tr)
    rd[...] = jnp.zeros_like(rd)
    S[0, own_rows, :] = s0[...]
    pl.semaphore_wait(barrier, rows + cols - 2)
    to_rows(lambda p: (S.at[0, own_rows], S.at[0, own_rows]), s_sem.at[0])

    def sum_cols(t):
        settle(PR.at[t, pl.ds(0, cols - 1)], p_sem.at[t, 1])
        QS[t] = jnp.sum(PR[t], axis=0)
        QR[t, r] = QS[t]
        to_rows(lambda p: (QS.at[t], QR.at[t, r]), q_sem.at[t])

    def sum_rows(t):
        settle(QR.at[t, pl.ds(0, rows - 1)], q_sem.at[t, 1])
        RO[t, own_k, :] = jnp.sum(QR[t], axis=0)
        to_cols(lambda p: (RO.at[t, own_k], RO.at[t, own_k]), r_sem.at[t])

    def slope(t):
        settle(F.at[t, pl.ds(0, cols - 1)], f_sem.at[t, 1])
        for cc in range(cols):
            f = F[t, cc].astype(F32)
            sl = f * (1.0 - f)
            for a in range(groups):
                SL[t, a * nb + cc * 8:a * nb + cc * 8 + 8, :] = sl[a * 8:a * 8 + 8]

    def learn(t):
        settle(RO.at[t, pl.ds(0, (cols - 1) * kp)], r_sem.at[t, 1])
        level = READ_DECAY * rd[...] + RO[t]
        rd[...] = level
        readout[t] = level.T
        err = jax.nn.sigmoid(level) - tgt[t]
        high = err.astype(BF16)
        low = (err - high.astype(F32)).astype(BF16)
        signal = jnp.dot(fbt[...], high, preferred_element_type=F32) + jnp.dot(fbt[...], low, preferred_element_type=F32)
        WG[t] = signal * SL[t]

    def step(t, _):
        settle(S.at[t, pl.ds(0, (rows - 1) * own)], s_sem.at[t, 1])
        ct = jnp.dot(wt[...], S[t], preferred_element_type=F32)
        CT[...] = ct
        for cc in range(cols):
            CS[t, cc] = jnp.concatenate(
                [ct[a * nb + cc * 8:a * nb + cc * 8 + 8] for a in range(groups)], axis=0).astype(BF16)
        to_cols(lambda p: (CS.at[t, p], CR.at[t, c]), c_sem.at[t])
        CR[t, c] = jnp.zeros((own, batch), BF16)

        @pl.when(t >= 1)
        def _():
            sum_cols(t - 1)
            slope(t - 1)

        @pl.when(t >= 2)
        def _():
            sum_rows(t - 2)

        now = LEAK * tr[...] + S[t].astype(F32)
        tr[...] = now
        TR[t] = now.astype(BF16)

        @pl.when(t >= 3)
        def _():
            learn(t - 3)

        settle(CR.at[t, pl.ds(0, cols - 1)], c_sem.at[t, 1])
        current = ext[t] + piece(CT) + jnp.sum(CR[t].astype(F32), axis=0)
        spike = S[t, own_rows, :].astype(F32)
        volt = LEAK * v[...] + current - spike
        adapt = d_own * u[...] + spike
        v[...] = volt
        u[...] = adapt
        rate = jax.nn.sigmoid(volt - 1.0 - g_own * adapt).astype(BF16)
        F[t, c] = rate

        @pl.when(t + 1 < steps)
        def _():
            S[t + 1, own_rows, :] = rate
            to_rows(lambda p: (S.at[t + 1, own_rows], S.at[t + 1, own_rows]), s_sem.at[t + 1])

        PS[t] = lax.dot_general(wo[...], rate, (((0,), (0,)), ((), ())), preferred_element_type=F32)
        to_cols(lambda p: (PS.at[t, pl.ds(pl.multiple_of(p * kp, kp), kp)], PR.at[t, c]), p_sem.at[t])
        PR[t, c] = PS[t, own_k, :]
        to_cols(lambda p: (F.at[t, c], F.at[t, c]), f_sem.at[t])
        return 0

    lax.fori_loop(0, steps, step, 0)
    last = steps - 1
    sum_cols(last)
    sum_rows(last - 1)
    slope(last)
    learn(last - 2)
    sum_rows(last)
    learn(last - 1)
    learn(last)

    chunk = min(64, nr)

    def back(i, _):
        at = pl.ds(pl.multiple_of(i * chunk, chunk), chunk)
        g, d = gain[at, :], decay[at, :]
        future = jnp.zeros((chunk, batch), F32)
        for t in reversed(range(steps)):
            w, sl = WG[t, at, :], SL[t, at, :]
            gs = g * sl
            FT[t, at, :] = (w - gs * future).astype(BF16)
            future = w + (d - gs) * future
        return 0

    lax.fori_loop(0, nr // chunk, back, 0)

    block = min(256, ns)
    sq[...] = jnp.zeros_like(sq)

    def grads(i, _):
        at = pl.ds(pl.multiple_of(i * block, block), block)
        lhs = jnp.concatenate([TR[t, at, :] for t in range(steps)], axis=1)
        rhs = jnp.concatenate([FT[t] for t in range(steps)], axis=1)
        out = lax.dot_general(lhs, rhs, (((1,), (1,)), ((), ())), preferred_element_type=F32)
        grad[at, :] = out
        two = jnp.sum((out * out).reshape(block // 8, 8, nr), axis=0)
        sq[...] += sum(two[:, i * 128:(i + 1) * 128] for i in range(nr // 128))
        return 0

    lax.fori_loop(0, ns // block, grads, 0)
    N1[r] = sq[...]
    to_rows(lambda p: (sq, N1.at[r]), n_sem.at[0])
    settle(N1.at[pl.ds(0, rows - 1)], n_sem.at[0, 1])
    settle(N1.at[pl.ds(0, rows - 1)], n_sem.at[0, 0])
    sq[...] = jnp.sum(N1[...], axis=0)
    N2[c] = sq[...]
    to_cols(lambda p: (sq, N2.at[c]), n_sem.at[1])
    settle(N2.at[pl.ds(0, cols - 1)], n_sem.at[1, 1])
    total = jnp.sum(jnp.sum(N2[...], axis=0), keepdims=True)
    factor = jnp.minimum(1.0, neurons / 16.0 / jnp.sqrt(total + 1e-06))
    clip[...] = jnp.broadcast_to(factor, clip.shape)

    def ends(t, _):
        settle(S.at[t, pl.ds(0, (rows - 1) * own)], s_sem.at[t, 0])
        settle(F.at[t, pl.ds(0, cols - 1)], f_sem.at[t, 0])
        settle(CR.at[t, pl.ds(0, cols - 1)], c_sem.at[t, 0])
        settle(PR.at[t, pl.ds(0, cols - 1)], p_sem.at[t, 0])
        settle(QR.at[t, pl.ds(0, rows - 1)], q_sem.at[t, 0])
        settle(RO.at[t, pl.ds(0, (cols - 1) * kp)], r_sem.at[t, 0])
        return 0

    lax.fori_loop(0, steps, ends, 0)
    settle(N2.at[pl.ds(0, cols - 1)], n_sem.at[1, 0])


def body(dims, inputs, targets, initial_spikes, w_in, w_rec, w_out, feedback, adapt_gain, adapt_decay):
    ny, nx, nz, nk, nb, steps, neurons = dims
    rows, cols = ny * nx, nz * nk
    batch, channels = inputs.shape[1:]
    own_cols, groups = w_rec.shape[1], w_rec.shape[2]
    own = groups * own_cols
    ns, nr = w_rec.shape[0] * own_cols, groups * nb
    kn = w_out.shape[2]
    kp = kn // cols
    start = lax.axis_index("col") * own_cols

    def part(array, dim):
        return lax.dynamic_slice_in_dim(array, start, own_cols, dim)

    wt = w_rec.reshape(ns, nr).T
    fbt = feedback.reshape(kn, nr).T
    gain = jnp.broadcast_to(adapt_gain.reshape(nr, 1), (nr, batch))
    decay = jnp.broadcast_to(adapt_decay.reshape(nr, 1), (nr, batch))
    s0 = part(initial_spikes, 2).reshape(batch, own).T.astype(BF16)
    wint = part(w_in, 2).reshape(channels, own).T
    inp = inputs.astype(BF16)
    tgt = targets.astype(F32).swapaxes(1, 2)
    wo = part(w_out, 1).reshape(own, kn)
    dma = pltpu.SemaphoreType.DMA
    V = pltpu.VMEM
    vm = pl.BlockSpec(memory_space=pltpu.VMEM)
    grad, readout, clip = pl.pallas_call(
        functools.partial(kernel, dims),
        out_shape=(
            jax.ShapeDtypeStruct((ns, nr), F32),
            jax.ShapeDtypeStruct((steps, batch, kn), F32),
            jax.ShapeDtypeStruct((8, 128), F32),
        ),
        in_specs=[vm] * 9,
        out_specs=(vm, vm, vm),
        scratch_shapes=[
            V((steps, ns, batch), BF16),
            V((steps, cols, own, batch), BF16),
            V((steps, cols, own, batch), BF16),
            V((steps, cols, own, batch), BF16),
            V((nr, batch), F32),
            V((steps, own, batch), F32),
            V((own, batch), F32),
            V((own, batch), F32),
            V((steps, kn, batch), F32),
            V((steps, cols, kp, batch), F32),
            V((steps, kp, batch), F32),
            V((steps, rows, kp, batch), F32),
            V((steps, kn, batch), F32),
            V((kn, batch), F32),
            V((steps, ns, batch), BF16),
            V((ns, batch), F32),
            V((steps, nr, batch), F32),
            V((steps, nr, batch), F32),
            V((steps, nr, batch), BF16),
            V((8, 128), F32),
            V((rows, 8, 128), F32),
            V((cols, 8, 128), F32),
            dma((steps, 2)), dma((steps, 2)), dma((steps, 2)), dma((steps, 2)), dma((steps, 2)), dma((steps, 2)),
            dma((2, 2)),
        ],
        compiler_params=pltpu.CompilerParams(
            collective_id=0, has_side_effects=True, vmem_limit_bytes=48 * 2**20
        ),
    )(wt, fbt, gain, decay, s0, wint, inp, tgt, wo)
    return readout, (grad * clip[0, 0]).reshape(w_rec.shape)


def build(mesh, split, na, nb, steps):
    dims = (*split, nb, steps, na * nb)
    placed = (
        P(),
        P(),
        P(None, "row", None),
        P(None, "row", None),
        P(None, "col", "row", None),
        P("row", None, None),
        P(None, "row", None),
        P("row", None),
        P("row", None),
    )
    return jax.shard_map(
        functools.partial(body, dims), mesh=mesh, in_specs=placed,
        out_specs=(P(), P(None, "col", "row", None)), check_vma=False,
    )


def solution(mesh):
    return build(mesh, (8, 4, 8, 2), 128, 128, 8)
```

time: 469 us -> 180 us (0.38)
  blocking collectives: 226 us -> 0 us
  Pallas kernels: 0 us -> 168 us
  waiting for transfers between devices: 136 us -> 0 us
  starting transfers between devices: 47.9 us -> 0 us
  between operations: 15 us -> 0.8 us
  local copies, waits for them, and re-layouts: 22 us -> 9.49 us
  matrix products: 10.9 us -> 0 us
  other arithmetic: 7.65 us -> 2.02 us
    all_to_all x11 -> x0, blocking collectives: 179 us -> none  [the longest x9 148 us: sent_to_all(): return lax.all_to_all(copies, axis, split_axis=0, concat_axis=0, tiled=True)]
    pallas_call x0 -> x1, Pallas kernels: none -> 168 us  [body(): pl.pallas_call(functools.partial(kernel, dims), out_shape=(jax.ShapeDtype...]
    all_to_all x9 -> x0, waiting for transfers between devices: 102 us -> none  [the longest x8 84.7 us: sum_at_owner(): lax.all_to_all(cut_along(array, dim, length), axis, 0, 0, tiled=True)]
    all_to_all x9 -> x0, starting transfers between devices: 47.8 us -> none  [the longest x8 39.1 us: sum_at_owner(): lax.all_to_all(cut_along(array, dim, length), axis, 0, 0, tiled=True)]
    psum x4 -> x0, blocking collectives: 47.7 us -> none  [by_axis(): return functools.reduce(lax.psum, axes, array)]
    all_gather x1 -> x0, waiting for transfers between devices: 34.3 us -> none  [body(): lax.all_gather(factors.reshape(rows_all, rows_loc, state_cols), COL, axis...]
    dot_general x13 -> x0, matrix products: 10.9 us -> none  [the longest x8 5.45 us: advance(): jnp.dot(arrivals, weights, preferred_element_type=jnp.float32)]
    dynamic_update_slice x16 -> x0, local copies, waits for them, and re-layouts: 6.95 us -> none  [body(): lax.scan(advance, (start_spikes, zeros, zeros, trace_zero), external)]
  transfers between devices with their start and end apart: 10 -> 0, of which waited for: 10 -> 0; matrix products, arithmetic and copies ran while one was open for 2% -> 0% of each run, Pallas kernels for 0% -> 0%
where the time goes in v1:
time: 180 us
  Pallas kernels  168 us (93%)
  local copies, waits for them, and re-layouts  9.49 us (5%)
  other arithmetic  2.02 us (1%)
    pallas_call x1, Pallas kernels, body(): pl.pallas_call(functools.partial(kernel, dims), out_shape=(jax.ShapeDtype...  168 us
    unnamed x16, local copies, waits for them, and re-layouts  5.16 us

profile of v1, /device:TPU:1, one launch (start us, length us, event | category | flops | bytes accessed | tf_op | source)
XLA Modules:
  0.0 180.2 jit_solution(1391525256147446625)
XLA Ops:
  0.6 0.0 copy-start
  0.6 0.0 copy-start.4
  0.7 0.0 copy-start.3
  0.7 0.0 copy-start.2
  0.7 0.8 dynamic-slice_bitcast_fusion.wo
  1.4 1.0 constant_dynamic-slice_fusion
  2.5 0.1 copy.26
  2.6 1.0 copy.24
  3.6 0.0 copy-done
  3.6 0.0 copy-start.1
  3.7 0.2 constant_dynamic-slice_fusion.1
  3.9 0.1 copy.29
  4.0 1.1 convert_element_type.16.inp
  5.1 0.0 copy-done.3
  5.1 0.1 broadcast_in_dim.15.gain
  5.2 0.0 copy-done.4
  5.2 0.1 broadcast_in_dim.17.decay
  5.3 0.0 copy-done.2
  5.4 0.2 copy.27
  5.6 0.0 copy-done.1
  5.6 1.2 copy.32
  6.8 1.5 copy.23
  8.3 167.9 %shard_map.104 = (f32[1024,512]{1,0:T(8,128)S(1)}, f32[8,128,128]{2,1,0:T(8,128)S(1)}, f32[8,128]{1,0:T(8,128)S(1)}) custom-call(bf16[512,1024]{1,0:T(8,128)(2,1)S(1)} %bitcast.25, bf16[512,128]{1,0:T(8,128)(2,1)S(1)} %bitcast.26, f32[512,128]{1,0:T(8,128)S(1)} %broadcast_in_dim.15.gain, f32[512,128]{1,0:T(8,128)S(1)} %broadcast_in_dim.17.decay, ...), custom_call_target="tpu_custom_call" | custom-call | tf_op jit(solution)/shard_map/pallas_call | solution.py:260
  176.2 0.5 slice.3
  176.7 0.9 multiply_bitcast_fusion
  177.6 1.9 %copy.28 = f32[128,8,4,128]{3,2,1,0:T(4,128)} copy(f32[128,8,4,128]{3,1,2,0:T(8,128)S(1)} %multiply_bitcast_fusion) | data formatting | bytes 4194304
  179.4 0.8 copy.34
  (2 shorter events, 0.0 us)
Async XLA Ops:
  0.6 3.0 %copy-start = (s32[128,4,128]{2,1,0:T(4,128)S(1)}, s32[128,4,128]{2,1,0:T(4,128)}, u32[]{:S(2)}) copy-start(s32[128,4,128]{2,1,0:T(4,128)} %param.11) | copy-start | bytes 786436
  0.6 4.6 %copy-start.4 = (f32[4,128]{1,0:T(4,128)S(1)}, f32[4,128]{1,0:T(4,128)}, u32[]{:S(2)}) copy-start(f32[4,128]{1,0:T(4,128)} %param.17) | copy-start | bytes 6148
  0.7 4.4 %copy-start.3 = (f32[4,128]{1,0:T(4,128)S(1)}, f32[4,128]{1,0:T(4,128)}, u32[]{:S(2)}) copy-start(f32[4,128]{1,0:T(4,128)} %param.16) | copy-start | bytes 6148
  0.7 4.7 %copy-start.2 = (s32[8,128,128]{2,1,0:T(8,128)S(1)}, s32[8,128,128]{2,1,0:T(8,128)}, u32[]{:S(2)}) copy-start(s32[8,128,128]{2,1,0:T(8,128)} %param.10) | copy-start | bytes 1572868
  3.6 2.0 %copy-start.1 = (bf16[128,8,4,128]{3,2,1,0:T(4,128)(2,1)S(1)}, bf16[128,8,4,128]{3,2,1,0:T(4,128)(2,1)}, u32[]{:S(2)}) copy-start(bf16[128,8,4,128]{3,2,1,0:T(4,128)(2,1)} %param.13) | copy-start | bytes 3145732

commit v2 on v1

v2 whole, which is shorter than its diff:
```python
import functools

import jax
import jax.numpy as jnp
from jax import lax
from jax.experimental import pallas as pl
from jax.experimental.pallas import tpu as pltpu
from jax.sharding import PartitionSpec as P

MESH = pl.DeviceIdType.MESH
LEAK = 0.8
READ_DECAY = 0.8
F32 = jnp.float32
BF16 = jnp.bfloat16


def rem(a, b):
    return a % b if isinstance(a, int) else lax.rem(a, jnp.int32(b))


def div(a, b):
    return a // b if isinstance(a, int) else lax.div(a, jnp.int32(b))


def outward(i, n):
    return n // 2 + (1 - 2 * rem(i, 2)) * div(i + 1, 2)


def kernel(dims, w_hbm, inp_hbm, tgt_hbm, s0_hbm, win_hbm, wo_hbm, fb_hbm, gain_hbm, decay_hbm, grad_hbm, levels_hbm, clip_hbm,
           grad, levels, clip,
           wb, wf, wt, inp, tgt, s0, small, wob, smallf, gain_ref, decay_ref, nat, fbt, winb, wok, gain, decay, ext,
           S, SR, F, CS, CR, CT, v, u, QS, QR, RO, rd, TR, tr, SL, WG, FT, sq, N1, N2,
           in_sem, s_sem, f_sem, c_sem, q_sem, r_sem, n_sem, out_sem):
    ny, nx, nz, nk, nb, steps, neurons = dims
    rows, cols = ny * nx, nz * nk
    r, c = lax.axis_index("row"), lax.axis_index("col")
    y, x, z, k = div(r, nx), rem(r, nx), div(c, nk), rem(c, nk)
    batch = inp.shape[1]
    half = batch // 2
    nr, ns = wt.shape
    kn = tgt.shape[2]
    kp = kn // cols
    groups = nr // nb
    own = groups * 8 // 2

    def row_peer(j):
        return rem(y + outward(div(j, nx), ny), ny) * nx + rem(x + outward(rem(j, nx), nx), nx)

    def col_peer(j):
        return rem(z + outward(div(j, nk), nz), nz) * nk + rem(k + outward(rem(j, nk), nk), nk)

    def to_rows(fn, sem):
        def one(j, _):
            p = row_peer(j)
            src, dst = fn(p)
            pltpu.make_async_remote_copy(src_ref=src, dst_ref=dst, send_sem=sem.at[0], recv_sem=sem.at[1],
                                         device_id=(p, c), device_id_type=MESH).start()
        for j in range(rows - 1):
            one(j, 0)

    def to_cols(fn, sem):
        def one(j, _):
            p = col_peer(j)
            src, dst = fn(p)
            pltpu.make_async_remote_copy(src_ref=src, dst_ref=dst, send_sem=sem.at[0], recv_sem=sem.at[1],
                                         device_id=(r, p), device_id_type=MESH).start()
        for j in range(cols - 1):
            one(j, 0)

    def settle(ref, sem):
        pltpu.make_async_copy(ref, ref, sem).wait()

    barrier = pltpu.get_barrier_semaphore()

    def greet_row(j, _):
        pl.semaphore_signal(barrier, inc=1, device_id=(row_peer(j), c), device_id_type=MESH)
        return 0

    def greet_col(j, _):
        pl.semaphore_signal(barrier, inc=1, device_id=(r, col_peer(j)), device_id_type=MESH)
        return 0

    lax.fori_loop(0, rows - 1, greet_row, 0)
    lax.fori_loop(0, cols - 1, greet_col, 0)
    loads = [pltpu.make_async_copy(src, dst, in_sem.at[i]) for i, (src, dst) in enumerate((
        (s0_hbm, s0), (win_hbm, small.at[0]), (inp_hbm, inp), (w_hbm, wb), (fb_hbm, small.at[1]), (wo_hbm, wob),
        (tgt_hbm, tgt), (gain_hbm, gain_ref), (decay_hbm, decay_ref)))]
    for load in loads:
        load.start()

    own_rows = pl.ds(pl.multiple_of(r * own, own), own)
    own_k = pl.ds(pl.multiple_of(c * kp, kp), kp)
    below_nb = lax.broadcasted_iota(jnp.int32, (nb, batch), 1) < half

    def turned(array):
        return pltpu.roll(array, half, 1)

    def paired(one, two):
        low = lax.broadcasted_iota(jnp.int32, one.shape, 1) < half
        return jnp.where(low, one, turned(two)), jnp.where(low, turned(one), two)

    def piece(ref):
        return jnp.concatenate([ref[pl.ds(pl.multiple_of(a * nb + c * 8, 8), 8), :] for a in range(groups)], axis=0)

    def packed(full):
        return paired(full[:own], full[own:])

    loads[0].wait()
    for a in range(groups):
        nat[a * nb:(a + 1) * nb, :] = s0[pl.ds(a, batch, stride=groups), :].astype(F32).T
    for p, tile in enumerate(packed(piece(nat))):
        S[0, p, own_rows, :] = tile.astype(BF16)
    pl.semaphore_wait(barrier, rows + cols - 2)
    for p in range(2):
        to_rows(lambda q: (S.at[0, p, own_rows], S.at[0, p, own_rows]), s_sem.at[0, p])

    loads[7].wait()
    loads[8].wait()
    for a in range(groups):
        at = slice(a * nb, (a + 1) * nb)
        gain[at, :] = jnp.broadcast_to(gain_ref[a:a + 1, :], (batch, nb)).T
        decay[at, :] = jnp.broadcast_to(decay_ref[a:a + 1, :], (batch, nb)).T
    g_own, d_own = packed(piece(gain)), packed(piece(decay))
    loads[1].wait()
    smallf[...] = small[0].astype(F32)
    for a in range(groups):
        nat[a * nb:(a + 1) * nb, :] = smallf[pl.ds(a, kn, stride=groups), :].T
    winb[...] = piece(nat).astype(BF16)
    loads[3].wait()
    part = wb.shape[0] // 8
    for i in range(8):
        wf[i * part:(i + 1) * part, :] = wb[i * part:(i + 1) * part, :].astype(F32)
    loads[2].wait()

    def outside(t, _):
        full = lax.dot_general(winb[...], inp[t].astype(F32).astype(BF16), (((1,), (1,)), ((), ())),
                               preferred_element_type=F32)
        one, two = packed(full)
        ext[t, 0], ext[t, 1] = one, two
        return 0

    lax.fori_loop(0, steps, outside, 0)
    for a in range(groups):
        wa = wf[pl.ds(a, ns, stride=groups), :].reshape(rows, 2, own, nb)
        for h in range(2):
            place = h if a < groups // 2 else 1 - h
            wt[a * nb:(a + 1) * nb, place * (ns // 2):(place + 1) * (ns // 2)] = (
                wa[:, h].reshape(ns // 2, nb).T.astype(BF16))
    loads[4].wait()
    smallf[...] = small[1].astype(F32)
    for a in range(groups):
        fbt[a * nb:(a + 1) * nb, :] = smallf[pl.ds(a, kn, stride=groups), :].T.astype(BF16)
    loads[5].wait()
    for a in range(groups):
        wok[:, a * nb:(a + 1) * nb] = wob[a * nb:(a + 1) * nb, :].astype(F32).T
    loads[6].wait()
    v[...] = jnp.zeros_like(v)
    u[...] = jnp.zeros_like(u)
    tr[...] = jnp.zeros_like(tr)
    rd[...] = jnp.zeros_like(rd)

    def drive(t, p):
        settle(S.at[t, p, pl.ds(0, (rows - 1) * own)], s_sem.at[t, p, 1])
        here = S[t, p]
        over = turned(here.astype(F32)).astype(BF16)
        SR[p] = over
        out = jnp.dot(wt[...], jnp.concatenate([here, over], axis=0), preferred_element_type=F32)
        for a in range(groups // 2):
            b = a + groups // 2
            CT[p, a * nb:(a + 1) * nb, :] = jnp.where(
                below_nb, out[a * nb:(a + 1) * nb], out[b * nb:(b + 1) * nb])
        for cc in range(cols):
            CS[t, p, cc] = jnp.concatenate(
                [CT[p, a * nb + cc * 8:a * nb + cc * 8 + 8, :] for a in range(groups // 2)], axis=0).astype(BF16)
        to_cols(lambda q: (CS.at[t, p, q], CR.at[t, p, c]), c_sem.at[t, p])
        CR[t, p, c] = jnp.zeros((own, batch), BF16)

    def move(t, p):
        mine = jnp.concatenate(
            [CT[p, pl.ds(pl.multiple_of(a * nb + c * 8, 8), 8), :] for a in range(groups // 2)], axis=0)
        spike = S[t, p, own_rows, :].astype(F32)
        kept = LEAK * v[p] + (ext[t, p] + mine) - spike
        adapt = d_own[p] * u[p] + spike
        u[p] = adapt
        settle(CR.at[t, p, pl.ds(0, cols - 1)], c_sem.at[t, p, 1])
        volt = kept + jnp.sum(CR[t, p].astype(F32), axis=0)
        v[p] = volt
        rate = jax.nn.sigmoid(volt - 1.0 - g_own[p] * adapt).astype(BF16)

        @pl.when(t + 1 < steps)
        def _():
            S[t + 1, p, own_rows, :] = rate
            to_rows(lambda q: (S.at[t + 1, p, own_rows], S.at[t + 1, p, own_rows]), s_sem.at[t + 1, p])

        F[t, c, p * own:(p + 1) * own, :] = rate

    def spread(t):
        to_cols(lambda q: (F.at[t, c], F.at[t, c]), f_sem.at[t])

    def project(t):
        settle(F.at[t, pl.ds(0, cols - 1)], f_sem.at[t, 1])
        halves = [F[t, :, p * own:(p + 1) * own, :].astype(F32).reshape(cols * own, batch) for p in range(2)]
        natural = []
        for full in paired(*halves):
            full = full.reshape(cols, groups // 2, 8, batch)
            natural += [full[:, a].reshape(nb, batch) for a in range(groups // 2)]
        QS[t] = jnp.dot(wok[own_k, :].astype(BF16), jnp.concatenate(natural, axis=0).astype(BF16),
                        preferred_element_type=F32)
        QR[t, r] = QS[t]
        to_rows(lambda q: (QS.at[t], QR.at[t, r]), q_sem.at[t])
        for a in range(groups):
            SL[t, a * nb:(a + 1) * nb, :] = natural[a] * (1.0 - natural[a])

    def gather(t):
        settle(QR.at[t, pl.ds(0, rows - 1)], q_sem.at[t, 1])
        RO[t, own_k, :] = jnp.sum(QR[t], axis=0)
        to_cols(lambda q: (RO.at[t, own_k], RO.at[t, own_k]), r_sem.at[t])

    def learn(t):
        settle(RO.at[t, pl.ds(0, (cols - 1) * kp)], r_sem.at[t, 1])
        level = READ_DECAY * rd[...] + RO[t]
        rd[...] = level
        err = jax.nn.sigmoid(level) - tgt[t].astype(F32).T
        high = err.astype(BF16)
        low = (err - high.astype(F32)).astype(BF16)
        signal = jnp.dot(fbt[...], high, preferred_element_type=F32) + jnp.dot(fbt[...], low, preferred_element_type=F32)
        WG[t] = signal * SL[t]
        levels[t] = level.T

    def trace(t):
        for h, full in enumerate((jnp.where(below_ns, S[t, 0].astype(F32), SR[1].astype(F32)),
                                  jnp.where(below_ns, SR[0].astype(F32), S[t, 1].astype(F32)))):
            now = LEAK * tr[h] + full
            tr[h] = now
            TR[t, :, h] = now.astype(BF16).reshape(rows, own, batch)

    below_ns = lax.broadcasted_iota(jnp.int32, (ns // 2, batch), 1) < half

    def step(t, _):
        drive(t, 0)
        drive(t, 1)
        trace(t)

        @pl.when(t >= 2)
        def _():
            gather(t - 2)

        move(t, 0)
        move(t, 1)
        spread(t)

        @pl.when(t >= 1)
        def _():
            project(t - 1)

        @pl.when(t >= 3)
        def _():
            learn(t - 3)
        return 0

    lax.fori_loop(0, steps, step, 0)
    last = steps - 1
    gather(last - 1)
    learn(last - 2)
    project(last)
    learn(last - 1)
    gather(last)
    learn(last)

    chunk = min(64, nr)

    def back(i, _):
        at = pl.ds(pl.multiple_of(i * chunk, chunk), chunk)
        g, d = gain[at, :], decay[at, :]
        future = jnp.zeros((chunk, batch), F32)
        for t in reversed(range(steps)):
            w, sl = WG[t, at, :], SL[t, at, :]
            gs = g * sl
            FT[t, at, :] = (w - gs * future).astype(BF16)
            future = w + (d - gs) * future
        return 0

    lax.fori_loop(0, nr // chunk, back, 0)

    block = min(8, rows)
    sq[...] = jnp.zeros_like(sq)

    def grads(i, _):
        at = pl.ds(i * block, block)
        count = block * 2 * own
        lhs = jnp.concatenate([TR[t, at].reshape(count, batch) for t in range(steps)], axis=1)
        rhs = jnp.concatenate([FT[t] for t in range(steps)], axis=1)
        out = lax.dot_general(lhs, rhs, (((1,), (1,)), ((), ())), preferred_element_type=F32)
        for a in range(groups):
            grad[pl.ds(i * (count * groups) + a, count, stride=groups), :] = out[:, a * nb:(a + 1) * nb]
        store = pl.ds(pl.multiple_of(i * (count * groups), count * groups), count * groups)
        pltpu.make_async_copy(grad.at[store], grad_hbm.at[store], out_sem.at[0]).start()
        two = jnp.sum((out * out).reshape(count // 8, 8, nr), axis=0)
        sq[...] += sum(two[:, i * nb:(i + 1) * nb] for i in range(groups))
        return 0

    pltpu.make_async_copy(levels, levels_hbm, out_sem.at[1]).start()
    lax.fori_loop(0, rows // block, grads, 0)
    N1[r] = sq[...]
    to_rows(lambda p: (sq, N1.at[r]), n_sem.at[0])
    settle(N1.at[pl.ds(0, rows - 1)], n_sem.at[0, 1])
    settle(N1.at[pl.ds(0, rows - 1)], n_sem.at[0, 0])
    sq[...] = jnp.sum(N1[...], axis=0)
    N2[c] = sq[...]
    to_cols(lambda p: (sq, N2.at[c]), n_sem.at[1])

    def ends(t, _):
        for p in range(2):
            settle(S.at[t, p, pl.ds(0, (rows - 1) * own)], s_sem.at[t, p, 0])
            settle(CR.at[t, p, pl.ds(0, cols - 1)], c_sem.at[t, p, 0])
        settle(F.at[t, pl.ds(0, cols - 1)], f_sem.at[t, 0])
        settle(QR.at[t, pl.ds(0, rows - 1)], q_sem.at[t, 0])
        settle(RO.at[t, pl.ds(0, (cols - 1) * kp)], r_sem.at[t, 0])
        return 0

    lax.fori_loop(0, steps, ends, 0)
    settle(N2.at[pl.ds(0, cols - 1)], n_sem.at[1, 1])
    settle(N2.at[pl.ds(0, cols - 1)], n_sem.at[1, 0])
    total = jnp.sum(jnp.sum(N2[...], axis=0), keepdims=True)
    factor = jnp.minimum(1.0, neurons / 16.0 / jnp.sqrt(total + 1e-06))
    clip[...] = jnp.broadcast_to(factor, clip.shape)
    pltpu.make_async_copy(clip, clip_hbm, out_sem.at[2]).start()
    settle(grad, out_sem.at[0])
    settle(levels, out_sem.at[1])
    settle(clip, out_sem.at[2])


def finish(levels_hbm, grad_hbm, clip_hbm, readout_hbm, scaled_hbm, grad, levels, clip, sem):
    parts = 4
    part = grad.shape[0] // parts
    at = [pl.ds(i * part, part) for i in range(parts)]
    bring = pltpu.make_async_copy(levels_hbm, levels, sem.at[2 * parts])
    last = pltpu.make_async_copy(levels, readout_hbm, sem.at[2 * parts + 2])
    factor = pltpu.make_async_copy(clip_hbm, clip, sem.at[2 * parts + 1])
    loads = [pltpu.make_async_copy(grad_hbm.at[at[i]], grad.at[at[i]], sem.at[i]) for i in range(parts)]
    stores = [pltpu.make_async_copy(grad.at[at[i]], scaled_hbm.at[at[i]], sem.at[parts + i]) for i in range(parts)]
    factor.start()
    for load in loads:
        load.start()
    bring.start()
    factor.wait()
    for i in range(parts):
        loads[i].wait()
        grad[at[i], :] = grad[at[i], :] * clip[0:1, :]
        stores[i].start()
    bring.wait()
    last.start()
    for store in stores:
        store.wait()
    last.wait()


def body(dims, inputs, targets, initial_spikes, w_in, w_rec, w_out, feedback, adapt_gain, adapt_decay):
    ny, nx, nz, nk, nb, steps, neurons = dims
    rows, cols = ny * nx, nz * nk
    batch, channels = inputs.shape[1:]
    own_cols, groups = w_rec.shape[1], w_rec.shape[2]
    own = groups * own_cols // 2
    ns, nr = w_rec.shape[0] * own_cols, groups * nb
    kn = w_out.shape[2]
    kp = kn // cols
    dma = pltpu.SemaphoreType.DMA
    V = pltpu.VMEM
    far = pl.BlockSpec(memory_space=pltpu.HBM)
    grad, levels, clip = pl.pallas_call(
        functools.partial(kernel, dims),
        out_shape=(
            jax.ShapeDtypeStruct((ns * groups, nb), F32),
            jax.ShapeDtypeStruct((steps, batch, kn), F32),
            jax.ShapeDtypeStruct((8, nb), F32),
        ),
        in_specs=[far] * 9,
        out_specs=(far, far, far),
        scratch_shapes=[
            V((ns * groups, nb), F32),
            V((steps, batch, kn), F32),
            V((8, nb), F32),
            V((ns * groups, nb), BF16),
            V((ns * groups, nb), F32),
            V((nr, ns), BF16),
            V((steps, batch, channels), jnp.int32),
            V((steps, batch, kn), jnp.int32),
            V((batch * groups, nb), jnp.int32),
            V((2, kn * groups, nb), BF16),
            V((nr, kn), BF16),
            V((kn * groups, nb), F32),
            V((groups, nb), F32),
            V((groups, nb), F32),
            V((nr, batch), F32),
            V((nr, kn), BF16),
            V((2 * own, channels), BF16),
            V((kn, nr), F32),
            V((nr, batch), F32),
            V((nr, batch), F32),
            V((steps, 2, own, batch), F32),
            V((steps, 2, rows * own, batch), BF16),
            V((2, rows * own, batch), BF16),
            V((steps, cols, 2 * own, batch), BF16),
            V((steps, 2, cols, own, batch), BF16),
            V((steps, 2, cols, own, batch), BF16),
            V((2, nr // 2, batch), F32),
            V((2, own, batch), F32),
            V((2, own, batch), F32),
            V((steps, kp, batch), F32),
            V((steps, rows, kp, batch), F32),
            V((steps, kn, batch), F32),
            V((kn, batch), F32),
            V((steps, rows, 2, own, batch), BF16),
            V((2, rows * own, batch), F32),
            V((steps, nr, batch), F32),
            V((steps, nr, batch), F32),
            V((steps, nr, batch), BF16),
            V((8, nb), F32),
            V((rows, 8, nb), F32),
            V((cols, 8, nb), F32),
            dma((9,)), dma((steps, 2, 2)), dma((steps, 2)), dma((steps, 2, 2)), dma((steps, 2)), dma((steps, 2)),
            dma((2, 2)), dma((3,)),
        ],
        compiler_params=pltpu.CompilerParams(
            collective_id=0, has_side_effects=True, vmem_limit_bytes=63 * 2**20
        ),
    )(w_rec.reshape(ns * groups, nb), inputs, targets, initial_spikes.reshape(batch * groups, nb),
      w_in.reshape(channels * groups, nb), w_out.reshape(nr, kn), feedback.reshape(kn * groups, nb), adapt_gain, adapt_decay)
    readout, scaled = pl.pallas_call(
        finish,
        out_shape=(
            jax.ShapeDtypeStruct((steps, batch, kn), F32),
            jax.ShapeDtypeStruct((ns * groups, nb), F32),
        ),
        in_specs=[far] * 3,
        out_specs=(far, far),
        scratch_shapes=[V((ns * groups, nb), F32), V((steps, batch, kn), F32), V((8, nb), F32), dma((11,))],
        compiler_params=pltpu.CompilerParams(vmem_limit_bytes=63 * 2**20),
    )(levels, grad, clip)
    return readout, scaled.reshape(w_rec.shape)


def build(mesh, split, na, nb, steps):
    dims = (*split, nb, steps, na * nb)
    placed = (
        P(),
        P(),
        P(None, "row", None),
        P(None, "row", None),
        P(None, "col", "row", None),
        P("row", None, None),
        P(None, "row", None),
        P("row", None),
        P("row", None),
    )
    return jax.shard_map(
        functools.partial(body, dims), mesh=mesh, in_specs=placed,
        out_specs=(P(), P(None, "col", "row", None)), check_vma=False,
    )


def solution(mesh):
    return build(mesh, (8, 4, 8, 2), 128, 128, 8)
```

time: 180 us -> 156 us (0.87)
  Pallas kernels: 168 us -> 155 us
  local copies, waits for them, and re-layouts: 9.49 us -> 0 us
  other arithmetic: 2.02 us -> 0 us
    pallas_call x1, Pallas kernels: 168 us -> 152 us  [body(): pl.pallas_call(functools.partial(kernel, dims), out_shape=(jax.ShapeDtype...]
    unnamed x16 -> x0, local copies, waits for them, and re-layouts: 5.16 us -> none
    pallas_call x0 -> x1, Pallas kernels: none -> 2.66 us  [body(): pl.pallas_call(finish, out_shape=(jax.ShapeDtypeStruct((steps, batch, kn)...]
    reshape x2 -> x0, local copies, waits for them, and re-layouts: 2.25 us -> none  [the longest x1 1.48 us: body(): wt = w_rec.reshape(ns, nr).T]
where the time goes in v2:
time: 156 us
  Pallas kernels  155 us (99%)
    pallas_call x1, Pallas kernels, body(): pl.pallas_call(functools.partial(kernel, dims), out_shape=(jax.ShapeDtype...  152 us

profile of v2, /device:TPU:1, one launch (start us, length us, event | category | flops | bytes accessed | tf_op | source)
XLA Modules:
  0.0 155.7 jit_solution(15620558876822919301)
XLA Ops:
  0.6 152.4 %shard_map.104 = (f32[4096,128]{1,0:T(8,128)}, f32[8,128,128]{2,1,0:T(8,128)}, f32[8,128]{1,0:T(8,128)}) custom-call(bf16[4096,128]{1,0:T(8,128)(2,1)} %bitcast.6, s32[8,128,128]{2,1,0:T(8,128)} %inp_hbm.1, s32[8,128,128]{2,1,0:T(8,128)} %tgt_hbm.1, s32[512,128]{1,0:T(8,128)} %bitcast.7, bf16[512,128]{1,0:T(8,128)(2,1)} %bitcast.8, ...), custom_call_target="tpu_custom_call" | custom-call | tf_op jit(solution)/shard_map/pallas_call | solution.py:370
  153.1 2.7 %shard_map.105 = (f32[8,128,128]{2,1,0:T(8,128)}, f32[4096,128]{1,0:T(8,128)}) custom-call(f32[8,128,128]{2,1,0:T(8,128)} %get-tuple-element.7.levels_hbm, f32[4096,128]{1,0:T(8,128)} %get-tuple-element.8.grad_hbm, f32[8,128]{1,0:T(8,128)} %get-tuple-element.9.clip_hbm), custom_call_target="tpu_custom_call" | custom-call | tf_op jit(solution)/shard_map/pallas_call | solution.py:429

commit v3 on v2

--- a/solution.py
+++ b/solution.py
@@ -29,7 +29,7 @@
 def kernel(dims, w_hbm, inp_hbm, tgt_hbm, s0_hbm, win_hbm, wo_hbm, fb_hbm, gain_hbm, decay_hbm, grad_hbm, levels_hbm, clip_hbm,
            grad, levels, clip,
            wb, wf, wt, inp, tgt, s0, small, wob, smallf, gain_ref, decay_ref, nat, fbt, winb, wok, gain, decay, ext,
-           S, SR, F, CS, CR, CT, v, u, QS, QR, RO, rd, TR, tr, SL, WG, FT, sq, N1, N2,
+           S, SR, F, CS, CR, CT, v, u, QS, QR, RO, rd, TR, tr, SL, WG, FT, sq, one, two, N1, N2,
            in_sem, s_sem, f_sem, c_sem, q_sem, r_sem, n_sem, out_sem):
     ny, nx, nz, nk, nb, steps, neurons = dims
     rows, cols = ny * nx, nz * nk
@@ -135,8 +135,7 @@
     def outside(t, _):
         full = lax.dot_general(winb[...], inp[t].astype(F32).astype(BF16), (((1,), (1,)), ((), ())),
                                preferred_element_type=F32)
-        one, two = packed(full)
-        ext[t, 0], ext[t, 1] = one, two
+        ext[t, 0], ext[t, 1] = packed(full)
         return 0
 
     lax.fori_loop(0, steps, outside, 0)
@@ -162,7 +161,7 @@
     def drive(t, p):
         settle(S.at[t, p, pl.ds(0, (rows - 1) * own)], s_sem.at[t, p, 1])
         here = S[t, p]
-        over = turned(here.astype(F32)).astype(BF16)
+        over = jnp.concatenate([here[:, half:], here[:, :half]], axis=1)
         SR[p] = over
         out = jnp.dot(wt[...], jnp.concatenate([here, over], axis=0), preferred_element_type=F32)
         for a in range(groups // 2):
@@ -192,7 +191,12 @@
             S[t + 1, p, own_rows, :] = rate
             to_rows(lambda q: (S.at[t + 1, p, own_rows], S.at[t + 1, p, own_rows]), s_sem.at[t + 1, p])
 
-        F[t, c, p * own:(p + 1) * own, :] = rate
+        mine = pl.ds(p * own, own)
+        F[t, c, mine, :] = rate
+
+        @pl.when(t + 1 == steps)
+        def _():
+            to_cols(lambda q: (F.at[t, c, mine], F.at[t, c, mine]), f_sem.at[t])
 
     def spread(t):
         to_cols(lambda q: (F.at[t, c], F.at[t, c]), f_sem.at[t])
@@ -236,32 +240,34 @@
 
     below_ns = lax.broadcasted_iota(jnp.int32, (ns // 2, batch), 1) < half
 
+    last = steps - 1
+
     def step(t, _):
         drive(t, 0)
         drive(t, 1)
+
+        @pl.when(t >= 1)
+        def _():
+            project(t - 1)
+
         trace(t)
-
-        @pl.when(t >= 2)
-        def _():
-            gather(t - 2)
-
         move(t, 0)
         move(t, 1)
-        spread(t)
+
+        @pl.when(t < last)
+        def _():
+            spread(t)
+
+        @pl.when(t >= 2)
+        def _():
+            learn(t - 2)
 
         @pl.when(t >= 1)
         def _():
-            project(t - 1)
-
-        @pl.when(t >= 3)
-        def _():
-            learn(t - 3)
+            gather(t - 1)
         return 0
 
     lax.fori_loop(0, steps, step, 0)
-    last = steps - 1
-    gather(last - 1)
-    learn(last - 2)
     project(last)
     learn(last - 1)
     gather(last)
@@ -295,19 +301,20 @@
             grad[pl.ds(i * (count * groups) + a, count, stride=groups), :] = out[:, a * nb:(a + 1) * nb]
         store = pl.ds(pl.multiple_of(i * (count * groups), count * groups), count * groups)
         pltpu.make_async_copy(grad.at[store], grad_hbm.at[store], out_sem.at[0]).start()
-        two = jnp.sum((out * out).reshape(count // 8, 8, nr), axis=0)
-        sq[...] += sum(two[:, i * nb:(i + 1) * nb] for i in range(groups))
+        squares = jnp.sum((out * out).reshape(count // 8, 8, nr), axis=0)
+        sq[...] += sum(squares[:, a * nb:(a + 1) * nb] for a in range(groups))
         return 0
 
     pltpu.make_async_copy(levels, levels_hbm, out_sem.at[1]).start()
     lax.fori_loop(0, rows // block, grads, 0)
-    N1[r] = sq[...]
-    to_rows(lambda p: (sq, N1.at[r]), n_sem.at[0])
+    one[...] = jnp.sum(sq[...], axis=0, keepdims=True)
+    N1[r] = one[...]
+    to_rows(lambda p: (one, N1.at[r]), n_sem.at[0])
     settle(N1.at[pl.ds(0, rows - 1)], n_sem.at[0, 1])
+    two[...] = jnp.sum(N1[...], axis=0)
+    N2[c] = two[...]
+    to_cols(lambda p: (two, N2.at[c]), n_sem.at[1])
     settle(N1.at[pl.ds(0, rows - 1)], n_sem.at[0, 0])
-    sq[...] = jnp.sum(N1[...], axis=0)
-    N2[c] = sq[...]
-    to_cols(lambda p: (sq, N2.at[c]), n_sem.at[1])
 
     def ends(t, _):
         for p in range(2):
@@ -416,8 +423,10 @@
             V((steps, nr, batch), F32),
             V((steps, nr, batch), BF16),
             V((8, nb), F32),
-            V((rows, 8, nb), F32),
-            V((cols, 8, nb), F32),
+            V((1, nb), F32),
+            V((1, nb), F32),
+            V((rows, 1, nb), F32),
+            V((cols, 1, nb), F32),
             dma((9,)), dma((steps, 2, 2)), dma((steps, 2)), dma((steps, 2, 2)), dma((steps, 2)), dma((steps, 2)),
             dma((2, 2)), dma((3,)),
         ],

time: 156 us -> 155 us (level)
  no operation moved by 1% of the time
where the time goes in v3:
time: 155 us; the launch traced here: 154 us
  Pallas kernels  154 us (99%)
    pallas_call x1, Pallas kernels, body(): pl.pallas_call(functools.partial(kernel, dims), out_shape=(jax.ShapeDtype...  151 us

profile of v3, /device:TPU:1, one launch (start us, length us, event | category | flops | bytes accessed | tf_op | source)
XLA Modules:
  0.0 154.4 jit_solution(6074189398093025990)
XLA Ops:
  0.6 151.1 %shard_map.104 = (f32[4096,128]{1,0:T(8,128)}, f32[8,128,128]{2,1,0:T(8,128)}, f32[8,128]{1,0:T(8,128)}) custom-call(bf16[4096,128]{1,0:T(8,128)(2,1)} %bitcast.6, s32[8,128,128]{2,1,0:T(8,128)} %inp_hbm.1, s32[8,128,128]{2,1,0:T(8,128)} %tgt_hbm.1, s32[512,128]{1,0:T(8,128)} %bitcast.7, bf16[512,128]{1,0:T(8,128)(2,1)} %bitcast.8, ...), custom_call_target="tpu_custom_call" | custom-call | tf_op jit(solution)/shard_map/pallas_call | solution.py:377
  151.7 2.7 %shard_map.105 = (f32[8,128,128]{2,1,0:T(8,128)}, f32[4096,128]{1,0:T(8,128)}) custom-call(f32[8,128,128]{2,1,0:T(8,128)} %get-tuple-element.7.levels_hbm, f32[4096,128]{1,0:T(8,128)} %get-tuple-element.8.grad_hbm, f32[8,128]{1,0:T(8,128)} %get-tuple-element.9.clip_hbm), custom_call_target="tpu_custom_call" | custom-call | tf_op jit(solution)/shard_map/pallas_call | solution.py:438
